TPU v7x, 128 devices: a whole 4x4x4 slice. The times are simulated.
128 devices in a mesh: layer: 4 (over z_lo, core), latent: 32 (over x, z_hi, y).
Axes of the slice: x: 4, y: 4, z: 4 (z_hi: 2, z_lo: 2; z = z_hi * 2 + z_lo), core: 2. Of those that a mesh axis runs over, the one named last changes fastest.
Arguments:
- residuals: bfloat16 [4, 512, 3584], P('layer', 'latent'), may hold values from -6 to 6
- enc_weight: bfloat16 [4, 3584, 24576], P('layer', None, 'latent'), may hold values from -0.046875 to 0.046875
- dec_weight: bfloat16 [4, 24576, 3584], P('layer', 'latent'), may hold values from -0.0390625 to 0.0390625
- enc_bias: float32 [24576], P('latent'), may hold values from -1 to 0.5
- dec_bias: float32 [4, 3584], P('layer'), may hold values from -3 to 3
Outputs:
- enc_grad: bfloat16 [4, 3584, 24576], P('layer', None, 'latent')
- dec_grad: bfloat16 [4, 24576, 3584], P('layer', 'latent')
- enc_bias_grad: float32 [24576], P('latent')
All inputs are finite; a program needn't handle non-finite values.
Results may differ from a plain program's by a relative error of at most 0.02.
Values may be sent and summed in bfloat16 or wider, within the bound.
No kernel may reach another device: no remote copies, remote signals or barrier semaphores. Data moves between devices by JAX's collectives and lax.ppermute only.
A program may use at most 128 MiB of HBM per device.

v0:
```python
import jax
import jax.numpy as jnp
from jax import lax
from jax.sharding import PartitionSpec as P

sparsity_weight = 0.5
sharpness = 4.0


def per_device(residuals, enc_weight, dec_weight, enc_bias, dec_bias):
    own_rows = residuals[0]
    enc_local = enc_weight[0]
    dec_local = dec_weight[0]
    gathered = lax.all_gather(own_rows, "latent", axis=0, tiled=True)
    pre_part = jnp.dot(gathered, enc_local, preferred_element_type=jnp.float32)
    row_norms = jnp.sqrt(jnp.sum(jnp.square(dec_local.astype(jnp.float32)), axis=1) + 1e-06)
    pre_total, weight_sum = lax.psum((pre_part, row_norms), "layer")
    pre_full = pre_total + enc_bias[None, :]
    latents = (jax.nn.softplus(sharpness * pre_full) / sharpness).astype(jnp.bfloat16)
    gate_all = jax.nn.sigmoid(sharpness * pre_full)
    act_sum = jnp.sum(latents.astype(jnp.float32), axis=0)
    lat_rows = latents
    rebuilt = lax.psum_scatter(
        jnp.dot(lat_rows, dec_local, preferred_element_type=jnp.float32).astype(jnp.bfloat16),
        "latent",
        scatter_dimension=0,
        tiled=True,
    ).astype(jnp.float32)
    misfit = rebuilt + dec_bias[0][None, :] - own_rows.astype(jnp.float32)
    err_grad = (2.0 * misfit).astype(jnp.bfloat16)
    err_piece = lax.all_gather(err_grad, "latent", axis=0, tiled=True)
    lat_rows = latents
    dec_acc = lax.dot_general(
        lat_rows, err_piece, (((0,), (0,)), ((), ())), preferred_element_type=jnp.float32
    )
    back_rows = lax.dot_general(
        err_piece, dec_local, (((1,), (1,)), ((), ())), preferred_element_type=jnp.float32
    )
    lat_part = back_rows
    dec_acc, lat_part = (dec_acc, lat_part)
    penalty = sparsity_weight * weight_sum[None, :]
    lat_grad = lax.psum(lat_part.astype(jnp.bfloat16), "layer").astype(jnp.float32) + penalty
    pre_grad = (lat_grad * gate_all).astype(jnp.bfloat16)
    enc_grad = lax.dot_general(
        gathered, pre_grad, (((0,), (0,)), ((), ())), preferred_element_type=jnp.float32
    ).astype(jnp.bfloat16)
    enc_bias_grad = jnp.sum(pre_grad.astype(jnp.float32), axis=0)
    penalty_term = (
        sparsity_weight * act_sum[:, None] * dec_local.astype(jnp.float32) / row_norms[:, None]
    )
    dec_grad = (dec_acc + penalty_term).astype(jnp.bfloat16)
    return (enc_grad[None], dec_grad[None], enc_bias_grad)


def solution(mesh):
    in_specs = (
        P("layer", "latent", None),
        P("layer", None, "latent"),
        P("layer", "latent", None),
        P("latent"),
        P("layer", None),
    )
    out_specs = (P("layer", None, "latent"), P("layer", "latent", None), P("latent"))
    return jax.shard_map(
        per_device, mesh=mesh, in_specs=in_specs, out_specs=out_specs, check_vma=False
    )
```

profile of v0, /device:TPU:1, one launch (start us, length us, event | category | flops | bytes accessed | tf_op | source)
XLA Modules:
  0.0 496.8 jit_solution(12142019913235078704)
XLA Ops:
  7.2 0.0 all-gather.6.cloned.1.call-start
  7.2 0.7 all-gather.6.cloned.1.call-update
  7.9 0.0 copy-start.2
  7.9 0.0 all-reduce.3.cloned.1.call-start
  8.0 84.8 %all-gather.6.cloned.1.call-done = bf16[1,512,3584]{2,1,0:T(8,128)(2,1)} async-done(((bf16[1,16,3584]{2,1,0:T(8,128)(2,1)}), bf16[1,512,3584]{2,1,0:T(8,128)(2,1)}) %all-gather.6.cloned.1.call-update) | async-done | bytes 3670032 | tf_op jit(solution)/shard_map/all_gather | solution.py:14
  92.7 7.8 %fusion.9 = f32[512,768]{1,0:T(8,128)} fusion(bf16[1,3584,768]{2,1,0:T(8,128)(2,1)} %param.6, bf16[1,512,3584]{2,1,0:T(8,128)(2,1)} %all-gather.6.cloned.1.call-done), kind=kOutput, calls=%fused_computation.13 | convolution fusion | flops 2818572288 | bytes 10747904 | tf_op jit(solution)/shard_map/dot_general | solution.py:15
  100.6 0.0 all-reduce.3.cloned.1.call-update
  100.6 0.0 reduce-scatter.2.cloned.1.call-start
  100.6 47.8 %all-reduce.3.cloned.1.call-done = f32[512,768]{1,0:T(8,128)} async-done(((f32[512,768]{1,0:T(8,128)}), f32[512,768]{1,0:T(8,128)}) %all-reduce.3.cloned.1.call-update) | async-done | bytes 1572880 | tf_op jit(solution)/shard_map/psum | solution.py:17
  148.5 0.0 copy-done.2
  148.5 2.6 convert_reduce_fusion.1
  151.0 7.0 %convolution_convert_fusion.1 = bf16[512,3584]{1,0:T(8,128)(2,1)} fusion(bf16[512,768]{1,0:T(8,128)(2,1)S(1)} %get-tuple-element.9, bf16[1,768,3584]{2,1,0:T(8,128)(2,1)} %param.7), kind=kOutput, calls=%fused_computation.9 | convolution fusion | flops 2820407296 | bytes 9961472 | tf_op jit(solution)/shard_map/dot_general | solution.py:24
  158.1 0.0 copy-start.3
  158.1 0.0 copy-start.1
  158.1 0.0 reduce-scatter.2.cloned.1.call-update
  158.1 0.0 all-gather.4.cloned.1.call-start
  158.1 0.6 copy-done.3
  158.8 168.0 %reduce-scatter.2.cloned.1.call-done = bf16[16,3584]{1,0:T(8,128)(2,1)} async-done(((bf16[512,3584]{1,0:T(8,128)(2,1)}), bf16[16,3584]{1,0:T(8,128)(2,1)}) %reduce-scatter.2.cloned.1.call-update) | async-done | bytes 114704 | tf_op jit(solution)/shard_map/reduce_scatter | solution.py:23
  326.8 0.0 copy-done.1
  326.8 1.6 fusion.19
  328.4 0.0 all-gather.4.cloned.1.call-update
  328.4 0.0 all-reduce.5.cloned.1.call-start
  328.5 3.7 fusion
  332.2 28.6 %psum.23 = f32[768]{0:T(1024)S(1)} all-reduce(f32[768]{0:T(1024)S(1)} %add_sqrt_fusion), channel_id=1, replica_groups=mesh['layer'=4,'latent'=32] {'layer'}, use_global_device_ids=true, to_apply=%region_4.5 | all-reduce | flops 768 | bytes 6144 | tf_op jit(solution)/shard_map/psum | solution.py:17
  360.8 66.0 %all-gather.4.cloned.1.call-done = bf16[512,3584]{1,0:T(8,128)(2,1)} async-done(((bf16[16,3584]{1,0:T(8,128)(2,1)}), bf16[512,3584]{1,0:T(8,128)(2,1)}) %all-gather.4.cloned.1.call-update) | async-done | bytes 3670032 | tf_op jit(solution)/shard_map/all_gather | solution.py:31
  426.8 7.6 %fusion.15 = bf16[512,768]{1,0:T(8,128)(2,1)} fusion(bf16[512,3584]{1,0:T(8,128)(2,1)} %all-gather.4.cloned.1.call-done, bf16[1,768,3584]{2,1,0:T(8,128)(2,1)} %param.7), kind=kOutput, calls=%fused_computation.24 | convolution fusion | flops 2818965504 | bytes 9961472 | tf_op jit(solution)/shard_map/dot_general | solution.py:36
  434.4 0.0 all-reduce.5.cloned.1.call-update
  434.4 0.0 copy-start
  434.4 8.4 %fusion.4 = bf16[1,768,3584]{2,1,0:T(8,128)(2,1)} fusion(bf16[512,768]{1,0:T(8,128)(2,1)S(1)} %get-tuple-element.9, bf16[512,3584]{1,0:T(8,128)(2,1)} %all-gather.4.cloned.1.call-done, bf16[1,768,3584]{2,1,0:T(8,128)(2,1)} %param.7, f32[768]{0:T(1024)S(1)} %add_sqrt_fusion, f32[768]{0:T(1024)S(1)} %broadcast_multiply_fusion), kind=kOutput, calls=%fused_computation.7 | convolution fusion | flops 2832334848 | bytes 15472640 | tf_op jit(solution)/shard_map/dot_general | solution.py:33
  442.9 29.9 %all-reduce.5.cloned.1.call-done = bf16[512,768]{1,0:T(8,128)(2,1)} async-done(((bf16[512,768]{1,0:T(8,128)(2,1)}), bf16[512,768]{1,0:T(8,128)(2,1)}) %all-reduce.5.cloned.1.call-update) | async-done | bytes 786448 | tf_op jit(solution)/shard_map/psum | solution.py:42
  472.8 0.0 copy-done
  472.8 2.3 convert_reduce_fusion
  475.1 6.9 %fusion.5 = bf16[1,3584,768]{1,2,0:T(8,128)(2,1)} fusion(bf16[512,768]{1,0:T(8,128)(2,1)S(1)} %get-tuple-element.7, bf16[1,512,3584]{2,1,0:T(8,128)(2,1)} %all-gather.6.cloned.1.call-done), kind=kOutput, calls=%fused_computation.8 | convolution fusion | flops 2821324800 | bytes 9961472 | tf_op jit(solution)/shard_map/dot_general | solution.py:44
  482.0 8.3 %copy.8 = bf16[1,3584,768]{2,1,0:T(8,128)(2,1)} copy(bf16[1,3584,768]{1,2,0:T(8,128)(2,1)} %fusion.5) | data formatting | bytes 11010048
  (4 shorter events, 0.1 us)
Async XLA Ops:
  7.2 85.6 %all-gather.6.cloned.1.call-start = ((), (), s32[]{:S(2)}) async-start(), calls=%async_computation.5 | async-start | bytes 3784704 | tf_op jit(solution)/shard_map/all_gather | solution.py:14
  7.9 140.6 %copy-start.2 = (f32[768]{0:T(1024)S(1)}, f32[768]{0:T(1024)}, u32[]{:S(2)}) copy-start(f32[768]{0:T(1024)} %param.8) | copy-start | bytes 9220
  7.9 140.6 %all-reduce.3.cloned.1.call-start = ((), (), s32[]{:S(2)}) async-start(), calls=%async_computation.1 | async-start | bytes 3145728 | tf_op jit(solution)/shard_map/psum | solution.py:17
  100.6 226.2 %reduce-scatter.2.cloned.1.call-start = ((), (), s32[]{:S(2)}) async-start(), calls=%async_computation.2 | async-start | bytes 3784704 | tf_op jit(solution)/shard_map/reduce_scatter | solution.py:23
  158.1 0.7 copy-start.3
  158.1 168.8 %copy-start.1 = (bf16[1,16,3584]{2,1,0:T(8,128)(2,1)S(1)}, bf16[1,16,3584]{2,1,0:T(8,128)(2,1)}, u32[]{:S(2)}) copy-start(bf16[1,16,3584]{2,1,0:T(8,128)(2,1)} %param.5) | copy-start | bytes 344068
  158.1 268.7 %all-gather.4.cloned.1.call-start = ((), (), s32[]{:S(2)}) async-start(), calls=%async_computation.3 | async-start | bytes 3784704 | tf_op jit(solution)/shard_map/all_gather | solution.py:31
  328.4 144.4 %all-reduce.5.cloned.1.call-start = ((), (), s32[]{:S(2)}) async-start(), calls=%async_computation.4 | async-start | bytes 1572864 | tf_op jit(solution)/shard_map/psum | solution.py:42
  434.4 38.4 %copy-start = (f32[512,768]{1,0:T(8,128)S(1)}, f32[512,768]{1,0:T(8,128)}, u32[]{:S(2)}) copy-start(f32[512,768]{1,0:T(8,128)} %all-reduce.3.cloned.1.call-done) | copy-start | bytes 4718596
Sparse Core Ops, SparseCore 0:
  11.0 81.7 all-gather.5
  100.7 47.7 all-reduce.2
  158.2 168.5 reduce-scatter.1
  330.7 96.1 all-gather.3
  434.6 38.1 all-reduce.4
where the time goes:
time: 497 us
  waiting for transfers between devices  397 us (80%)
  matrix products  37.7 us (8%)
  blocking collectives  28.6 us (6%)
  between operations  13.8 us (3%)
  other arithmetic  10.2 us (2%)
  local copies, waits for them, and re-layouts  8.91 us (2%)
    reduce_scatter x1, waiting for transfers between devices, per_device(): lax.psum_scatter(jnp.dot(lat_rows, dec_local, preferred_element_type=jnp....  168 us
    all_gather x1, waiting for transfers between devices, per_device(): gathered = lax.all_gather(own_rows, 'latent', axis=0, tiled=True)  84.8 us
    all_gather x1, waiting for transfers between devices, per_device(): err_piece = lax.all_gather(err_grad, 'latent', axis=0, tiled=True)  66 us
    psum x1, waiting for transfers between devices, per_device(): pre_total, weight_sum = lax.psum((pre_part, row_norms), 'layer')  47.8 us
    psum x1, waiting for transfers between devices, per_device(): lax.psum(lat_part.astype(jnp.bfloat16), 'layer').astype(jnp.float32)  29.9 us
    psum x1, blocking collectives, per_device(): pre_total, weight_sum = lax.psum((pre_part, row_norms), 'layer')  28.6 us
  transfers between devices with their start and end apart: 5, of which 5 were waited for; matrix products, arithmetic and copies ran while one was open for 2% of the time, Pallas kernels for 0%

commit v1 on v0

--- a/solution.py
+++ b/solution.py
@@ -11,7 +11,9 @@
     own_rows = residuals[0]
     enc_local = enc_weight[0]
     dec_local = dec_weight[0]
-    gathered = lax.all_gather(own_rows, "latent", axis=0, tiled=True)
+    gathered = jnp.concatenate(
+        lax.all_to_all(jnp.stack([own_rows] * lax.axis_size("latent")), "latent", 0, 0), axis=0
+    )
     pre_part = jnp.dot(gathered, enc_local, preferred_element_type=jnp.float32)
     row_norms = jnp.sqrt(jnp.sum(jnp.square(dec_local.astype(jnp.float32)), axis=1) + 1e-06)
     pre_total, weight_sum = lax.psum((pre_part, row_norms), "layer")

time: 497 us -> 467 us (0.940)
  waiting for transfers between devices: 397 us -> 312 us
  blocking collectives: 28.6 us -> 84.8 us
    all_gather x1 -> x0, waiting for transfers between devices: 84.8 us -> none  [per_device(): gathered = lax.all_gather(own_rows, 'latent', axis=0, tiled=True)]
    all_to_all x0 -> x1, blocking collectives: none -> 56.2 us  [per_device(): lax.all_to_all(jnp.stack([own_rows] * lax.axis_size('latent')), 'latent',...]
    unnamed x9 -> x13, local copies, waits for them, and re-layouts: 8.91 us -> 10.8 us
  transfers between devices with their start and end apart: 5 -> 4, of which waited for: 5 -> 4; matrix products, arithmetic and copies ran while one was open for 2% -> 3% of each run, Pallas kernels for 0% -> 0%
where the time goes in v1:
time: 467 us
  waiting for transfers between devices  312 us (67%)
  blocking collectives  84.8 us (18%)
  matrix products  34 us (7%)
  between operations  13.8 us (3%)
  local copies, waits for them, and re-layouts  12.1 us (3%)
  other arithmetic  10.2 us (2%)
    reduce_scatter x1, waiting for transfers between devices, per_device(): lax.psum_scatter(jnp.dot(lat_rows, dec_local, preferred_element_type=jnp....  168 us
    all_gather x1, waiting for transfers between devices, per_device(): err_piece = lax.all_gather(err_grad, 'latent', axis=0, tiled=True)  66.2 us
    all_to_all x1, blocking collectives, per_device(): lax.all_to_all(jnp.stack([own_rows] * lax.axis_size('latent')), 'latent',...  56.2 us
    psum x1, waiting for transfers between devices, per_device(): pre_total, weight_sum = lax.psum((pre_part, row_norms), 'layer')  47.5 us
    psum x1, waiting for transfers between devices, per_device(): lax.psum(lat_part.astype(jnp.bfloat16), 'layer').astype(jnp.float32)  30 us
    psum x1, blocking collectives, per_device(): pre_total, weight_sum = lax.psum((pre_part, row_norms), 'layer')  28.6 us
    unnamed x13, local copies, waits for them, and re-layouts  10.8 us
  transfers between devices with their start and end apart: 4, of which 4 were waited for; matrix products, arithmetic and copies ran while one was open for 3% of the time, Pallas kernels for 0%

profile of v1, /device:TPU:1, one launch (start us, length us, event | category | flops | bytes accessed | tf_op | source)
XLA Modules:
  0.0 466.7 jit_solution(15551952564110971701)
XLA Ops:
  7.2 0.0 all-reduce.3.cloned.1.call-start
  7.2 1.3 stack.3
  8.5 0.0 copy-start.5
  8.5 56.2 %all_to_all.5 = bf16[32,16,3584]{2,1,0:T(8,128)(2,1)S(1)} all-to-all(bf16[32,16,3584]{2,1,0:T(8,128)(2,1)S(1)} %stack.3), channel_id=1, replica_groups=mesh['layer'=4,'latent'=32] {'latent'}, dimensions={0} | all-to-all | bytes 7340032 | tf_op jit(solution)/shard_map/all_to_all | solution.py:15
  64.7 0.0 copy-start.1
  64.7 1.8 copy-done.1
  66.5 0.0 copy-done.5
  66.5 0.0 copy-start.3
  66.6 4.1 fusion.9
  70.7 0.0 all-reduce.3.cloned.1.call-update
  70.7 0.0 reduce-scatter.2.cloned.1.call-start
  70.8 47.5 %all-reduce.3.cloned.1.call-done = f32[512,768]{1,0:T(8,128)} async-done(((f32[512,768]{1,0:T(8,128)}), f32[512,768]{1,0:T(8,128)}) %all-reduce.3.cloned.1.call-update) | async-done | bytes 1572880 | tf_op jit(solution)/shard_map/psum | solution.py:19
  118.2 0.0 copy-done.3
  118.2 2.6 convert_reduce_fusion.1
  120.8 7.0 %convolution_convert_fusion.1 = bf16[512,3584]{1,0:T(8,128)(2,1)} fusion(bf16[512,768]{1,0:T(8,128)(2,1)S(1)} %get-tuple-element.9, bf16[1,768,3584]{2,1,0:T(8,128)(2,1)} %param.7), kind=kOutput, calls=%fused_computation.9 | convolution fusion | flops 2820407296 | bytes 9961472 | tf_op jit(solution)/shard_map/dot_general | solution.py:26
  127.8 0.0 copy-start.4
  127.8 0.0 copy-start.2
  127.8 0.0 reduce-scatter.2.cloned.1.call-update
  127.8 0.0 all-gather.2.cloned.1.call-start
  127.9 0.6 copy-done.4
  128.5 168.0 %reduce-scatter.2.cloned.1.call-done = bf16[16,3584]{1,0:T(8,128)(2,1)} async-done(((bf16[512,3584]{1,0:T(8,128)(2,1)}), bf16[16,3584]{1,0:T(8,128)(2,1)}) %reduce-scatter.2.cloned.1.call-update) | async-done | bytes 114704 | tf_op jit(solution)/shard_map/reduce_scatter | solution.py:25
  296.6 0.0 copy-done.2
  296.6 1.6 multiply_convert_fusion.1
  298.2 0.0 all-gather.2.cloned.1.call-update
  298.2 0.0 all-reduce.5.cloned.1.call-start
  298.2 3.7 fusion
  301.9 28.6 %psum.23 = f32[768]{0:T(1024)S(1)} all-reduce(f32[768]{0:T(1024)S(1)} %add_sqrt_fusion), channel_id=1, replica_groups=mesh['layer'=4,'latent'=32] {'layer'}, use_global_device_ids=true, to_apply=%region_4.5 | all-reduce | flops 768 | bytes 6144 | tf_op jit(solution)/shard_map/psum | solution.py:19
  330.5 66.2 %all-gather.2.cloned.1.call-done = bf16[512,3584]{1,0:T(8,128)(2,1)} async-done(((bf16[16,3584]{1,0:T(8,128)(2,1)}), bf16[512,3584]{1,0:T(8,128)(2,1)}) %all-gather.2.cloned.1.call-update) | async-done | bytes 3670032 | tf_op jit(solution)/shard_map/all_gather | solution.py:33
  396.7 7.6 %fusion.13 = bf16[512,768]{1,0:T(8,128)(2,1)} fusion(bf16[512,3584]{1,0:T(8,128)(2,1)} %all-gather.2.cloned.1.call-done, bf16[1,768,3584]{2,1,0:T(8,128)(2,1)} %param.7), kind=kOutput, calls=%fused_computation.22 | convolution fusion | flops 2818965504 | bytes 9961472 | tf_op jit(solution)/shard_map/dot_general | solution.py:38
  404.3 0.0 all-reduce.5.cloned.1.call-update
  404.3 0.0 copy-start
  404.4 8.4 %fusion.4 = bf16[1,768,3584]{2,1,0:T(8,128)(2,1)} fusion(bf16[512,768]{1,0:T(8,128)(2,1)S(1)} %get-tuple-element.9, bf16[512,3584]{1,0:T(8,128)(2,1)} %all-gather.2.cloned.1.call-done, bf16[1,768,3584]{2,1,0:T(8,128)(2,1)} %param.7, f32[768]{0:T(1024)S(1)} %add_sqrt_fusion, f32[768]{0:T(1024)S(1)} %broadcast_multiply_fusion), kind=kOutput, calls=%fused_computation.7 | convolution fusion | flops 2832334848 | bytes 15472640 | tf_op jit(solution)/shard_map/dot_general | solution.py:35
  412.8 30.0 %all-reduce.5.cloned.1.call-done = bf16[512,768]{1,0:T(8,128)(2,1)} async-done(((bf16[512,768]{1,0:T(8,128)(2,1)}), bf16[512,768]{1,0:T(8,128)(2,1)}) %all-reduce.5.cloned.1.call-update) | async-done | bytes 786448 | tf_op jit(solution)/shard_map/psum | solution.py:44
  442.8 0.0 copy-done
  442.8 2.3 convert_reduce_fusion
  445.0 6.9 %fusion.5 = bf16[1,3584,768]{1,2,0:T(8,128)(2,1)} fusion(bf16[512,768]{1,0:T(8,128)(2,1)S(1)} %get-tuple-element.7, bf16[512,3584]{1,0:T(8,128)(2,1)} %bitcast.29), kind=kOutput, calls=%fused_computation.8 | convolution fusion | flops 2821324800 | bytes 9961472 | tf_op jit(solution)/shard_map/dot_general | solution.py:46
  451.9 8.3 %copy.8 = bf16[1,3584,768]{2,1,0:T(8,128)(2,1)} copy(bf16[1,3584,768]{1,2,0:T(8,128)(2,1)} %fusion.5) | data formatting | bytes 11010048
  (4 shorter events, 0.1 us)
Async XLA Ops:
  7.2 111.1 %all-reduce.3.cloned.1.call-start = ((), (), s32[]{:S(2)}) async-start(), calls=%async_computation.2 | async-start | bytes 3145728 | tf_op jit(solution)/shard_map/psum | solution.py:19
  8.5 58.0 %copy-start.5 = (bf16[1,3584,768]{2,1,0:T(8,128)(2,1)S(1)}, bf16[1,3584,768]{2,1,0:T(8,128)(2,1)}, u32[]{:S(2)}) copy-start(bf16[1,3584,768]{2,1,0:T(8,128)(2,1)} %param.6) | copy-start | bytes 16515076
  64.7 1.8 copy-start.1
  66.5 51.7 %copy-start.3 = (f32[768]{0:T(1024)S(1)}, f32[768]{0:T(1024)}, u32[]{:S(2)}) copy-start(f32[768]{0:T(1024)} %param.8) | copy-start | bytes 9220
  70.7 225.8 %reduce-scatter.2.cloned.1.call-start = ((), (), s32[]{:S(2)}) async-start(), calls=%async_computation.3 | async-start | bytes 3784704 | tf_op jit(solution)/shard_map/reduce_scatter | solution.py:25
  127.8 0.7 copy-start.4
  127.8 168.8 %copy-start.2 = (bf16[1,16,3584]{2,1,0:T(8,128)(2,1)S(1)}, bf16[1,16,3584]{2,1,0:T(8,128)(2,1)}, u32[]{:S(2)}) copy-start(bf16[1,16,3584]{2,1,0:T(8,128)(2,1)} %param.5) | copy-start | bytes 344068
  127.8 268.9 %all-gather.2.cloned.1.call-start = ((), (), s32[]{:S(2)}) async-start(), calls=%async_computation.4 | async-start | bytes 3784704 | tf_op jit(solution)/shard_map/all_gather | solution.py:33
  298.2 144.6 %all-reduce.5.cloned.1.call-start = ((), (), s32[]{:S(2)}) async-start(), calls=%async_computation.5 | async-start | bytes 1572864 | tf_op jit(solution)/shard_map/psum | solution.py:44
  404.3 38.4 %copy-start = (f32[512,768]{1,0:T(8,128)S(1)}, f32[512,768]{1,0:T(8,128)}, u32[]{:S(2)}) copy-start(f32[512,768]{1,0:T(8,128)} %all-reduce.3.cloned.1.call-done) | copy-start | bytes 4718596
Sparse Core Ops, SparseCore 0:
  70.8 47.3 all-reduce.2
  127.9 168.5 reduce-scatter.1
  300.5 96.1 all-gather.1
  404.5 38.2 all-reduce.4
